TPU v7x, 256 devices: a whole 4x4x8 slice. The times are simulated.
256 devices in a mesh: replica: 32 (over x, z), shard: 8 (over y, core).
Axes of the slice: x: 4, y: 4, z: 8, core: 2. Of those that a mesh axis runs over, the one named last changes fastest.
Arguments:
- grads: bfloat16 [32, 8192, 2048], P('replica', 'shard'), may hold values from -64 to 64
- errors: bfloat16 [32, 8192, 2048], P('replica', 'shard'), may hold values from -4 to 4
- q_prev: bfloat16 [32, 2048], P(None, 'shard'), may hold values from -6 to 6
- momentum: float32 [8192, 2048], P('shard', 'replica'), may hold values from -1.2 to 1.2
Outputs:
- new_errors: bfloat16 [32, 8192, 2048], P('replica', 'shard')
- new_momentum: float32 [8192, 2048], P('shard', 'replica')
- q_next: float32 [32, 2048], P(None, 'shard')
All inputs are finite; a program needn't handle non-finite values.
Results may differ from a plain program's by a relative error of at most 0.012.
Values may be sent and summed in bfloat16 or wider, within the bound.
A program may use at most 64 MiB of HBM per device.

v0:
```python
import jax
import jax.numpy as jnp
from jax import lax
from jax.sharding import PartitionSpec as P


def shards(grads, errors, q_prev, momentum):
    highest = lax.Precision.HIGHEST
    merged = grads[0].astype(jnp.float32) + errors[0].astype(jnp.float32)
    col_count = merged.shape[1]
    product = lax.dot_general(
        merged,
        lax.all_gather(q_prev, "shard", axis=1, tiled=True).astype(jnp.float32),
        (((1,), (1,)), ((), ())),
        precision=highest,
    )
    factor = lax.psum(product.astype(jnp.bfloat16), "replica").astype(jnp.float32)
    every_row = lax.all_gather(factor.astype(jnp.bfloat16), "shard", axis=0, tiled=True).astype(
        factor.dtype
    )
    gram_matrix = jnp.dot(every_row.T, every_row, precision=highest)
    lower_factor = jnp.linalg.cholesky(gram_matrix)
    ortho = jax.scipy.linalg.solve_triangular(lower_factor, factor.T, lower=True).T
    right_term = jnp.dot(ortho.T, merged, precision=highest)
    replicas = lax.axis_size("replica")
    block_width = col_count // lax.axis_size("shard")
    right_full = lax.psum(right_term, ("replica", "shard")) / replicas
    q_next = lax.dynamic_slice_in_dim(
        right_full, lax.axis_index("shard") * block_width, block_width, 1
    )
    approx = jnp.dot(ortho, right_full, precision=highest)
    new_errors = (merged - approx).astype(jnp.bfloat16)[None]
    momentum_width = momentum.shape[1]
    approx_block = lax.dynamic_slice_in_dim(
        approx, lax.axis_index("replica") * momentum_width, momentum_width, 1
    )
    new_momentum = 0.9 * momentum + approx_block
    return (new_errors, new_momentum, q_next)


def solution(mesh):
    return jax.shard_map(
        shards,
        mesh=mesh,
        in_specs=(
            P("replica", "shard", None),
            P("replica", "shard", None),
            P(None, "shard"),
            P("shard", "replica"),
        ),
        out_specs=(P("replica", "shard", None), P("shard", "replica"), P(None, "shard")),
        check_vma=False,
    )
```

profile of v0, /device:TPU:2, one launch (start us, length us, event | category | flops | bytes accessed | tf_op | source)
XLA Modules:
  0.0 478.8 jit_solution(6031099820396762904)
XLA Ops:
  7.2 0.0 all-reduce.3.cloned.1.call-start
  7.2 13.5 %all_gather.6 = bf16[32,2048]{1,0:T(8,128)(2,1)S(1)} all-gather(bf16[32,256]{1,0:T(8,128)(2,1)} %param.6), channel_id=1, replica_groups=mesh['replica'=32,'shard'=8] {'shard'}, dimensions={1}, use_global_device_ids=true | all-gather | bytes 147456 | tf_op jit(solution)/shard_map/all_gather | solution.py:13
  20.7 0.0 copy-start.2
  20.7 9.1 %fusion.6 = bf16[1024,32]{0,1:T(8,128)(2,1)} fusion(bf16[32,2048]{1,0:T(8,128)(2,1)S(1)} %all_gather.6, bf16[1,1024,2048]{2,1,0:T(8,128)(2,1)} %param.5, bf16[1,1024,2048]{2,1,0:T(8,128)(2,1)} %param.4), kind=kOutput, calls=%fused_computation.8 | convolution fusion | flops 811630592 | bytes 8585216 | tf_op jit(solution)/shard_map/dot_general | solution.py:11
  29.8 0.0 all-reduce.3.cloned.1.call-update
  29.8 0.0 all-reduce.5.cloned.1.call-start
  29.8 141.3 %all-reduce.3.cloned.1.call-done = bf16[1024,32]{0,1:T(8,128)(2,1)} async-done(((bf16[1024,32]{0,1:T(8,128)(2,1)}), bf16[1024,32]{0,1:T(8,128)(2,1)}) %all-reduce.3.cloned.1.call-update) | async-done | bytes 65552 | tf_op jit(solution)/shard_map/psum | solution.py:17
  171.2 13.8 %all_gather.7 = bf16[8192,32]{0,1:T(8,128)(2,1)S(1)} all-gather(bf16[1024,32]{0,1:T(8,128)(2,1)} %all-reduce.3.cloned.1.call-done), channel_id=1, replica_groups=mesh['replica'=32,'shard'=8] {'shard'}, dimensions={0}, use_global_device_ids=true | all-gather | bytes 589824 | tf_op jit(solution)/shard_map/all_gather | solution.py:18
  185.0 0.3 fusion.14
  185.3 0.1 copy.7
  185.4 2.9 cholesky.16
  188.3 0.6 compare_reduce_fusion
  189.0 0.7 fusion.9
  189.6 2.4 custom-call.7
  192.1 1.1 fusion.10
  193.2 8.6 %fusion = f32[32,2048]{1,0:T(8,128)} fusion(f32[32,1024]{1,0:T(8,128)S(1)} %fusion.10, bf16[1,1024,2048]{2,1,0:T(8,128)(2,1)} %param.5, bf16[1,1024,2048]{2,1,0:T(8,128)(2,1)} %param.4), kind=kOutput, calls=%fused_computation.1 | convolution fusion | flops 811597824 | bytes 8781824 | tf_op jit(solution)/shard_map/dot_general | solution.py:24
  201.7 0.0 all-reduce.5.cloned.1.call-update
  201.8 0.0 copy-done.2
  201.8 0.2 copy.8
  202.0 248.0 %all-reduce.5.cloned.1.call-done = f32[32,2048]{1,0:T(8,128)} async-done(((f32[32,2048]{1,0:T(8,128)}), f32[32,2048]{1,0:T(8,128)}) %all-reduce.5.cloned.1.call-update) | async-done | bytes 262160 | tf_op jit(solution)/shard_map/psum | solution.py:27
  450.0 0.0 copy-start
  450.0 10.0 %fusion.13 = f32[1024,2048]{1,0:T(8,128)} fusion(f32[32,1024]{1,0:T(8,128)S(1)} %fusion.10, f32[32,2048]{1,0:T(8,128)} %all-reduce.5.cloned.1.call-done), kind=kOutput, calls=%fused_computation.22 | convolution fusion | flops 805371904 | bytes 8781824 | tf_op jit(solution)/shard_map/dot_general | solution.py:31
  459.9 0.0 copy-done
  459.9 0.0 copy-start.1
  459.9 9.2 %fusion.5 = bf16[1,1024,2048]{2,1,0:T(8,128)(2,1)} fusion(f32[1024,2048]{1,0:T(8,128)} %fusion.13, bf16[1,1024,2048]{2,1,0:T(8,128)(2,1)S(1)} %copy-done, bf16[1,1024,2048]{2,1,0:T(8,128)(2,1)} %param.4), kind=kLoop, calls=%fused_computation.7 | loop fusion | flops 10485760 | bytes 20971520 | tf_op jit(solution)/shard_map/broadcast_in_dim | solution.py:32
  469.2 1.2 dynamic-slice_add_fusion
  470.4 0.9 copy.9
  471.3 0.0 copy-done.1
  471.3 0.6 constant_dynamic-slice_fusion
  (3 shorter events, 0.1 us)
Async XLA Ops:
  7.2 164.0 %all-reduce.3.cloned.1.call-start = ((), (), s32[]{:S(2)}) async-start(), calls=%async_computation | async-start | bytes 131072 | tf_op jit(solution)/shard_map/psum | solution.py:17
  20.7 181.1 %copy-start.2 = (f32[1024,64]{0,1:T(8,128)S(1)}, f32[1024,64]{0,1:T(8,128)}, u32[]{:S(2)}) copy-start(f32[1024,64]{0,1:T(8,128)} %param.7) | copy-start | bytes 786436
  29.8 420.2 %all-reduce.5.cloned.1.call-start = ((), (), s32[]{:S(2)}) async-start(), calls=%async_computation.1 | async-start | bytes 524288 | tf_op jit(solution)/shard_map/psum | solution.py:27
  450.0 10.0 %copy-start = (bf16[1,1024,2048]{2,1,0:T(8,128)(2,1)S(1)}, bf16[1,1024,2048]{2,1,0:T(8,128)(2,1)}, u32[]{:S(2)}) copy-start(bf16[1,1024,2048]{2,1,0:T(8,128)(2,1)} %param.5) | copy-start | bytes 12582916
  459.9 11.4 %copy-start.1 = (f32[32,2048]{1,0:T(8,128)S(1)}, f32[32,2048]{1,0:T(8,128)}, u32[]{:S(2)}) copy-start(f32[32,2048]{1,0:T(8,128)} %all-reduce.5.cloned.1.call-done) | copy-start | bytes 786436
Sparse Core Ops, SparseCore 0:
  29.9 141.2 all-reduce.2
  201.9 248.0 all-reduce.4
where the time goes:
time: 479 us
  waiting for transfers between devices  389 us (81%)
  matrix products  29 us (6%)
  blocking collectives  27.3 us (6%)
  other arithmetic  17.2 us (4%)
  between operations  14.1 us (3%)
    psum x1, waiting for transfers between devices, shards(): right_full = lax.psum(right_term, ('replica', 'shard')) / replicas  248 us
    psum x1, waiting for transfers between devices, shards(): lax.psum(product.astype(jnp.bfloat16), 'replica').astype(jnp.float32)  141 us
    all_gather x1, blocking collectives, shards(): lax.all_gather(factor.astype(jnp.bfloat16), 'shard', axis=0, tiled=True)  13.8 us
    all_gather x1, blocking collectives, shards(): lax.all_gather(q_prev, 'shard', axis=1, tiled=True).astype(jnp.float32)  13.5 us
    dot_general x1, matrix products, shards(): approx = jnp.dot(ortho, right_full, precision=highest)  9.98 us
  transfers between devices with their start and end apart: 2, of which 2 were waited for; matrix products, arithmetic and copies ran while one was open for 0% of the time, Pallas kernels for 0%

commit v1 on v0

--- a/solution.py
+++ b/solution.py
@@ -24,7 +24,7 @@
     right_term = jnp.dot(ortho.T, merged, precision=highest)
     replicas = lax.axis_size("replica")
     block_width = col_count // lax.axis_size("shard")
-    right_full = lax.psum(right_term, ("replica", "shard")) / replicas
+    right_full = lax.psum(lax.psum(right_term, "shard"), "replica") / replicas
     q_next = lax.dynamic_slice_in_dim(
         right_full, lax.axis_index("shard") * block_width, block_width, 1
     )

time: 479 us -> 440 us (0.919)
  waiting for transfers between devices: 389 us -> 350 us
    psum x1 -> x2, waiting for transfers between devices: 248 us -> 208 us  [shards(): right_full = lax.psum(lax.psum(right_term, 'shard'), 'replica') / replicas]
  transfers between devices with their start and end apart: 2 -> 3, of which waited for: 2 -> 3; matrix products, arithmetic and copies ran while one was open for 0% -> 0% of each run, Pallas kernels for 0% -> 0%
where the time goes in v1:
time: 440 us; the launch traced here: 439 us
  waiting for transfers between devices  350 us (80%)
  matrix products  29 us (7%)
  blocking collectives  27.1 us (6%)
  other arithmetic  17.2 us (4%)
  between operations  13.8 us (3%)
    psum x2, waiting for transfers between devices, shards(): right_full = lax.psum(lax.psum(right_term, 'shard'), 'replica') / replicas  208 us
    psum x1, waiting for transfers between devices, shards(): lax.psum(product.astype(jnp.bfloat16), 'replica').astype(jnp.float32)  141 us
    all_gather x1, blocking collectives, shards(): lax.all_gather(factor.astype(jnp.bfloat16), 'shard', axis=0, tiled=True)  13.6 us
    all_gather x1, blocking collectives, shards(): lax.all_gather(q_prev, 'shard', axis=1, tiled=True).astype(jnp.float32)  13.5 us
    dot_general x1, matrix products, shards(): approx = jnp.dot(ortho, right_full, precision=highest)  9.98 us
    broadcast_in_dim x1, other arithmetic, shards(): new_errors = (merged - approx).astype(jnp.bfloat16)[None]  9.22 us
    dot_general x1, matrix products, shards(): lax.dot_general(merged, lax.all_gather(q_prev, 'shard', axis=1, tiled=Tru...  9.05 us
  transfers between devices with their start and end apart: 3, of which 3 were waited for; matrix products, arithmetic and copies ran while one was open for 0% of the time, Pallas kernels for 0%

profile of v1, /device:TPU:2, one launch (start us, length us, event | category | flops | bytes accessed | tf_op | source)
XLA Modules:
  0.0 438.9 jit_solution(9595012559058689329)
XLA Ops:
  7.2 0.0 all-reduce.4.cloned.1.call-start
  7.2 13.5 %all_gather.6 = bf16[32,2048]{1,0:T(8,128)(2,1)S(1)} all-gather(bf16[32,256]{1,0:T(8,128)(2,1)} %param.6), channel_id=1, replica_groups=mesh['replica'=32,'shard'=8] {'shard'}, dimensions={1}, use_global_device_ids=true | all-gather | bytes 147456 | tf_op jit(solution)/shard_map/all_gather | solution.py:13
  20.7 0.0 copy-start.2
  20.7 9.1 %fusion.6 = bf16[1024,32]{0,1:T(8,128)(2,1)} fusion(bf16[32,2048]{1,0:T(8,128)(2,1)S(1)} %all_gather.6, bf16[1,1024,2048]{2,1,0:T(8,128)(2,1)} %param.5, bf16[1,1024,2048]{2,1,0:T(8,128)(2,1)} %param.4), kind=kOutput, calls=%fused_computation.8 | convolution fusion | flops 811630592 | bytes 8585216 | tf_op jit(solution)/shard_map/dot_general | solution.py:11
  29.8 0.0 all-reduce.4.cloned.1.call-update
  29.8 0.0 all-reduce.6.cloned.1.call-start
  29.8 141.3 %all-reduce.4.cloned.1.call-done = bf16[1024,32]{0,1:T(8,128)(2,1)} async-done(((bf16[1024,32]{0,1:T(8,128)(2,1)}), bf16[1024,32]{0,1:T(8,128)(2,1)}) %all-reduce.4.cloned.1.call-update) | async-done | bytes 65552 | tf_op jit(solution)/shard_map/psum | solution.py:17
  171.2 13.6 %all_gather.7 = bf16[8192,32]{0,1:T(8,128)(2,1)S(1)} all-gather(bf16[1024,32]{0,1:T(8,128)(2,1)} %all-reduce.4.cloned.1.call-done), channel_id=1, replica_groups=mesh['replica'=32,'shard'=8] {'shard'}, dimensions={0}, use_global_device_ids=true | all-gather | bytes 589824 | tf_op jit(solution)/shard_map/all_gather | solution.py:18
  184.8 0.3 fusion.14
  185.1 0.1 copy.7
  185.2 2.9 cholesky.16
  188.1 0.6 compare_reduce_fusion
  188.8 0.7 fusion.9
  189.4 2.4 custom-call.7
  191.9 1.1 fusion.10
  193.0 8.6 %fusion = f32[32,2048]{1,0:T(8,128)} fusion(f32[32,1024]{1,0:T(8,128)S(1)} %fusion.10, bf16[1,1024,2048]{2,1,0:T(8,128)(2,1)} %param.5, bf16[1,1024,2048]{2,1,0:T(8,128)(2,1)} %param.4), kind=kOutput, calls=%fused_computation.1 | convolution fusion | flops 811597824 | bytes 8781824 | tf_op jit(solution)/shard_map/dot_general | solution.py:24
  201.6 0.0 all-reduce.6.cloned.1.call-update
  201.6 0.2 all-reduce.8.cloned.1.call-start
  201.8 62.7 %all-reduce.6.cloned.1.call-done = f32[32,2048]{1,0:T(8,128)} async-done(((f32[32,2048]{1,0:T(8,128)}), f32[32,2048]{1,0:T(8,128)}) %all-reduce.6.cloned.1.call-update) | async-done | bytes 262160 | tf_op jit(solution)/shard_map/psum | solution.py:27
  264.5 0.0 all-reduce.8.cloned.1.call-update
  264.5 0.0 copy-done.2
  264.5 0.2 copy.8
  264.7 145.7 %all-reduce.8.cloned.1.call-done = f32[32,2048]{1,0:T(8,128)} async-done(((f32[32,2048]{1,0:T(8,128)}), f32[32,2048]{1,0:T(8,128)}) %all-reduce.8.cloned.1.call-update) | async-done | bytes 262160 | tf_op jit(solution)/shard_map/psum | solution.py:27
  410.4 0.0 copy-start
  410.4 10.0 %fusion.13 = f32[1024,2048]{1,0:T(8,128)} fusion(f32[32,1024]{1,0:T(8,128)S(1)} %fusion.10, f32[32,2048]{1,0:T(8,128)} %all-reduce.8.cloned.1.call-done), kind=kOutput, calls=%fused_computation.22 | convolution fusion | flops 805371904 | bytes 8781824 | tf_op jit(solution)/shard_map/dot_general | solution.py:31
  420.4 0.0 copy-done
  420.4 0.0 copy-start.1
  420.4 9.2 %fusion.5 = bf16[1,1024,2048]{2,1,0:T(8,128)(2,1)} fusion(f32[1024,2048]{1,0:T(8,128)} %fusion.13, bf16[1,1024,2048]{2,1,0:T(8,128)(2,1)S(1)} %copy-done, bf16[1,1024,2048]{2,1,0:T(8,128)(2,1)} %param.4), kind=kLoop, calls=%fused_computation.7 | loop fusion | flops 10485760 | bytes 20971520 | tf_op jit(solution)/shard_map/broadcast_in_dim | solution.py:32
  429.6 1.2 dynamic-slice_add_fusion
  430.8 0.9 copy.9
  431.7 0.0 copy-done.1
  431.7 0.6 constant_dynamic-slice_fusion
  (3 shorter events, 0.1 us)
Async XLA Ops:
  7.2 164.0 %all-reduce.4.cloned.1.call-start = ((), (), s32[]{:S(2)}) async-start(), calls=%async_computation | async-start | bytes 131072 | tf_op jit(solution)/shard_map/psum | solution.py:17
  20.7 243.8 %copy-start.2 = (f32[1024,64]{0,1:T(8,128)S(1)}, f32[1024,64]{0,1:T(8,128)}, u32[]{:S(2)}) copy-start(f32[1024,64]{0,1:T(8,128)} %param.7) | copy-start | bytes 786436
  29.8 234.7 %all-reduce.6.cloned.1.call-start = ((), (), s32[]{:S(2)}) async-start(), calls=%async_computation.1 | async-start | bytes 524288 | tf_op jit(solution)/shard_map/psum | solution.py:27
  201.6 208.8 %all-reduce.8.cloned.1.call-start = ((), (), s32[]{:S(2)}) async-start(), calls=%async_computation.2 | async-start | bytes 524288 | tf_op jit(solution)/shard_map/psum | solution.py:27
  410.4 10.0 %copy-start = (bf16[1,1024,2048]{2,1,0:T(8,128)(2,1)S(1)}, bf16[1,1024,2048]{2,1,0:T(8,128)(2,1)}, u32[]{:S(2)}) copy-start(bf16[1,1024,2048]{2,1,0:T(8,128)(2,1)} %param.5) | copy-start | bytes 12582916
  420.4 11.4 %copy-start.1 = (f32[32,2048]{1,0:T(8,128)S(1)}, f32[32,2048]{1,0:T(8,128)}, u32[]{:S(2)}) copy-start(f32[32,2048]{1,0:T(8,128)} %all-reduce.8.cloned.1.call-done) | copy-start | bytes 786436
Sparse Core Ops, SparseCore 0:
  29.9 141.2 all-reduce.3
  201.7 62.7 all-reduce.5
  268.3 142.0 all-reduce.7
